TPU v7x, 32 devices: a whole 2x2x4 slice. The times are simulated.
32 devices in a mesh: step: 4 (over z), band: 8 (over y, x, core).
Axes of the slice: x: 2, y: 2, z: 4, core: 2. Of those that a mesh axis runs over, the one named last changes fastest.
Arguments:
- states: float32 [4, 16, 10752], P('step', 'band'), may hold values from -6 to 6
- anchor: float32 [16, 10752], P('band'), may hold values from -6 to 6
- step_index: int32 [4], P('step'), may hold values from 0 to 19
- sigmas: float32 [20], replicated, may hold values from 0.05 to 0.5
- enc_w: bfloat16 [84, 512], replicated, may hold values from -0.625 to 0.625
- noise_embed: float32 [512], replicated, may hold values from -3 to 3
- qkv_w: bfloat16 [512, 1536], replicated, may hold values from -0.25 to 0.25
- out_w: bfloat16 [512, 512], replicated, may hold values from -0.25 to 0.25
- up_w: bfloat16 [512, 1024], replicated, may hold values from -0.25 to 0.25
- down_w: bfloat16 [1024, 512], replicated, may hold values from -0.1875 to 0.1875
- dec_w: bfloat16 [512, 84], replicated, may hold values from -0.25 to 0.25
Outputs:
- new_states: float32 [4, 16, 10752], P('step', 'band')
- change: float32 [4], P('step')
All inputs are finite; a program needn't handle non-finite values.
Results may differ from a plain program's by a relative error of at most 0.0031.
Values may be sent and summed in bfloat16 or wider, within the bound.
A program may use at most 64 MiB of HBM per device.

v0:
```python
import math

import jax
import jax.numpy as jnp
from jax import lax
from jax.sharding import PartitionSpec as P

C = 84
W = 512
HEADS = 4
HEAD_DIM = 128
LEVELS = 20
R = 2


epsilon = 1e-06
score_gain = 3.0


def passed_along(array, axis, by):
    length = lax.axis_size(axis)
    pairs = [(i, i + by) for i in range(length) if 0 <= i + by < length]
    return lax.ppermute(array, axis, pairs)


def with_halo(array, sides, width):
    for axis, dim in sides:
        size, length = (lax.axis_size(axis), array.shape[dim])
        up = [(i, (i + 1) % size) for i in range(size - 1)]
        down = [(j, i) for i, j in up]
        last = lax.slice_in_dim(array, length - width, length, axis=dim)
        initial = lax.slice_in_dim(array, 0, width, axis=dim)
        before = lax.ppermute(last, axis, up)
        after = lax.ppermute(initial, axis, down)
        array = jnp.concatenate([before, array, after], axis=dim)
    return array


def carried_in(part, axis, combine, identity):
    place = lax.axis_index(axis)
    gathered = lax.all_gather(part, axis)
    state = jnp.zeros_like(part) + jnp.asarray(identity, part.dtype)

    def one(turn, state):
        return combine(state, lax.dynamic_index_in_dim(gathered, turn, 0, False))

    return lax.fori_loop(0, place, one, state)


def rms_scale(values):
    return values * lax.rsqrt(jnp.mean(values * values, axis=-1, keepdims=True) + epsilon)


def split_heads(projected):
    heads = rms_scale(projected.reshape(projected.shape[0], HEADS, HEAD_DIM))
    return heads.astype(jnp.bfloat16)


def embed_rows(fields, enc_w, offset_vec):
    tokens = fields.reshape(-1, C)
    embedded = jnp.dot(tokens, enc_w, preferred_element_type=jnp.float32) + offset_vec[None, :]
    return (embedded, rms_scale(embedded).astype(jnp.bfloat16))


def window_mask_for(first_row, lat_rows, total_rows):
    offsets = jnp.arange(lat_rows + 2 * R, dtype=jnp.int32) - R
    key_rows = first_row + offsets
    inside = (key_rows >= 0) & (key_rows < total_rows)
    near = jnp.abs(jnp.arange(lat_rows, dtype=jnp.int32)[:, None] - offsets[None, :]) <= R
    return (inside[None, :] & near).astype(jnp.float32)


def attend(queries, key_heads, value_heads, window_mask):
    scores = jnp.einsum("qhd,khd->hqk", queries, key_heads, preferred_element_type=jnp.float32)
    scores = scores * (score_gain / math.sqrt(HEAD_DIM))
    heads, count_q, count_k = scores.shape
    rows_q = window_mask.shape[0]
    rows_k = window_mask.shape[1]
    columns = count_q // rows_q
    weights = jnp.exp(scores).reshape(heads, rows_q, columns, rows_k, columns)
    weights = (weights * window_mask[None, :, None, :, None]).reshape(heads, count_q, count_k)
    softmax_weights = (weights / jnp.sum(weights, axis=-1, keepdims=True)).astype(jnp.bfloat16)
    attended = jnp.einsum(
        "hqk,khd->qhd", softmax_weights, value_heads, preferred_element_type=jnp.float32
    )
    return attended.astype(jnp.bfloat16).reshape(count_q, W)


def finish_block(embedded, attended, out_w, up_w, down_w, dec_w):
    mixed = embedded + jnp.dot(attended, out_w, preferred_element_type=jnp.float32)
    normed = rms_scale(mixed).astype(jnp.bfloat16)
    hidden = jax.nn.gelu(jnp.dot(normed, up_w, preferred_element_type=jnp.float32)).astype(
        jnp.bfloat16
    )
    mixed = mixed + jnp.dot(hidden, down_w, preferred_element_type=jnp.float32)
    return jnp.dot(rms_scale(mixed).astype(jnp.bfloat16), dec_w, preferred_element_type=jnp.float32)


def add_fields(earlier, later):
    return earlier + later


def local(
    states, anchor, step_index, sigmas, enc_w, noise_embed, qkv_w, out_w, up_w, down_w, dec_w
):
    steps_here, lat_rows, field_width = states.shape
    columns = field_width // C
    total_rows = lat_rows * lax.axis_size("band")
    first_row = lax.axis_index("band") * lat_rows
    previous = passed_along(states.astype(jnp.bfloat16), "step", 1).astype(states.dtype)
    opening = jnp.where(lax.axis_index("step") == 0, anchor[None], previous)
    inputs = jnp.concatenate([opening, states[:-1]], axis=0)
    onehot = (step_index[:, None] == jnp.arange(LEVELS, dtype=jnp.int32)[None, :]).astype(
        jnp.float32
    )
    noise_levels = jnp.sum(onehot * sigmas[None, :], axis=1)
    fields = inputs.astype(jnp.bfloat16)
    window_mask = window_mask_for(first_row, lat_rows, total_rows)
    widened = with_halo(fields, (("band", 1),), R)
    offset_vec = jnp.log(noise_levels[0]) * noise_embed
    embedded, normed = embed_rows(widened[0], enc_w, offset_vec)
    key_value = jnp.dot(normed, qkv_w[:, W:], preferred_element_type=jnp.float32)
    key_heads = split_heads(key_value[:, :W])
    value_heads = key_value[:, W:].astype(jnp.bfloat16).reshape(-1, HEADS, HEAD_DIM)
    center_normed = normed[R * columns : (R + lat_rows) * columns]
    queries = split_heads(jnp.dot(center_normed, qkv_w[:, :W], preferred_element_type=jnp.float32))
    attended = attend(queries, key_heads, value_heads, window_mask)
    center_embed = embedded[R * columns : (R + lat_rows) * columns]
    drift_list = [finish_block(center_embed, attended, out_w, up_w, down_w, dec_w)]
    drifts = jnp.stack(
        [drift_rows.reshape(lat_rows, field_width) for drift_rows in drift_list], axis=0
    )
    running = jnp.cumsum(noise_levels[:, None, None] * drifts, axis=0)
    block_total = running[-1]
    earlier = carried_in(block_total, "step", add_fields, jnp.zeros_like(block_total))
    new_states = anchor[None] + (earlier[None] + running)
    latitude = (
        jnp.pi
        * ((first_row + jnp.arange(lat_rows, dtype=jnp.int32)).astype(jnp.float32) + 0.5)
        / total_rows
        - 0.5 * jnp.pi
    )
    area = jnp.cos(latitude)
    all_latitude = jnp.pi * ((jnp.arange(total_rows, dtype=jnp.float32) + 0.5) / total_rows - 0.5)
    area_total = jnp.sum(jnp.cos(all_latitude))
    mismatch = new_states - states
    partial_value = jnp.sum(area[None, :, None] * mismatch * mismatch, axis=(1, 2))
    change = lax.psum(partial_value, "band") / (area_total * field_width)
    return (new_states, change)


def solution(mesh):
    placed = (
        P("step", "band", None),
        P("band", None),
        P("step"),
        P(),
        P(),
        P(),
        P(),
        P(),
        P(),
        P(),
        P(),
    )
    return jax.shard_map(
        local,
        mesh=mesh,
        in_specs=placed,
        out_specs=(P("step", "band", None), P("step")),
        check_vma=False,
    )
```

profile of v0, /device:TPU:0, one launch (start us, length us, event | category | flops | bytes accessed | tf_op | source)
XLA Modules:
  0.0 70.2 jit_solution(570986452210668265)
XLA Ops:
  0.6 1.0 %convert_element_type.52 = bf16[1,2,10752]{2,1,0:T(2,128)(2,1)S(1)} convert(f32[1,2,10752]{2,1,0:T(2,128)} %param.13) | non-fusion elementwise | flops 21504 | bytes 129024 | tf_op jit(solution)/shard_map/convert_element_type | solution.py:110
  1.7 4.9 %collective-permute-start = (bf16[1,2,10752]{2,1,0:T(2,128)(2,1)S(1)}, bf16[1,2,10752]{2,1,0:T(2,128)(2,1)S(1)}, u32[]{:S(2)}, u32[]{:S(2)}) collective-permute-start(bf16[1,2,10752]{2,1,0:T(2,128)(2,1)S(1)} %convert_element_type.52), channel_id=1, source_target_pairs={{0,8},{8,16},{16,24},{1,9},{9,17},{17,25},{2,10},{10,18},{18,26},{... | collective-permute-start | bytes 129032 | tf_op jit(solution)/shard_map/ppermute | solution.py:23
  7.3 1.3 %fusion.30 = f32[]{:T(128)} fusion(f32[20]{0:T(128)} %param.16, s32[]{:T(128)} %bitcast.34), kind=kLoop, calls=%fused_computation.61 | loop fusion | flops 59 | bytes 88 | tf_op jit(solution)/shard_map/reduce_sum | solution.py:116
  9.2 0.7 broadcast_multiply_fusion
  9.9 0.9 %fusion.29 = bf16[1,2,10752]{2,1,0:T(2,128)(2,1)S(1)} fusion(f32[2,10752]{1,0:T(2,128)} %param.14, bf16[1,2,10752]{2,1,0:T(2,128)(2,1)S(1)} %collective-permute-done, pred[]{:T(512)S(6)} %eq.17), kind=kLoop, calls=%fused_computation.52 | loop fusion | flops 43008 | bytes 172033 | tf_op jit(solution)/shard_map/convert_element_type | solution.py:117
  10.9 1.3 %collective-permute-start.2 = (bf16[1,2,10752]{2,1,0:T(2,128)(2,1)S(1)}, bf16[1,2,10752]{2,1,0:T(2,128)(2,1)S(1)}, u32[]{:S(2)}, u32[]{:S(2)}) collective-permute-start(bf16[1,2,10752]{2,1,0:T(2,128)(2,1)S(1)} %fusion.29), channel_id=1, source_target_pairs={{1,0},{2,1},{3,2},{4,3},{5,4},{6,5},{7,6},{9,8},{10,9},{11,10},{12... | collective-permute-start | bytes 129032 | tf_op jit(solution)/shard_map/ppermute | solution.py:34
  12.2 3.0 %collective-permute-start.1 = (bf16[1,2,10752]{2,1,0:T(2,128)(2,1)S(1)}, bf16[1,2,10752]{2,1,0:T(2,128)(2,1)S(1)}, u32[]{:S(2)}, u32[]{:S(2)}) collective-permute-start(bf16[1,2,10752]{2,1,0:T(2,128)(2,1)S(1)} %fusion.29), channel_id=1, source_target_pairs={{0,1},{1,2},{2,3},{3,4},{4,5},{5,6},{6,7},{8,9},{9,10},{10,11},{11... | collective-permute-start | bytes 129032 | tf_op jit(solution)/shard_map/ppermute | solution.py:33
  15.3 0.3 mul.164
  15.7 1.1 %copy.41 = f32[256,768]{1,0:T(8,128)} copy(f32[256,768]{0,1:T(8,128)S(1)} %bitcast.36) | data formatting | bytes 1572864 | tf_op jit(solution)/shard_map/mul | solution.py:81
  16.8 0.7 cosine_reduce_fusion
  18.3 0.6 reshape_squeeze.3
  19.0 0.4 multiply_reduce_fusion.1
  19.6 1.0 %copy-done.1 = f32[768,512]{0,1:T(8,128)} copy-done((f32[768,512]{0,1:T(8,128)}, f32[768,512]{0,1:T(8,128)S(1)}, u32[]{:S(2)}) %copy-start.1) | copy-done | bytes 1572888
  20.6 0.8 %copy-done.4 = bf16[512,1536]{1,0:T(8,128)(2,1)S(1)} copy-done((bf16[512,1536]{1,0:T(8,128)(2,1)S(1)}, bf16[512,1536]{1,0:T(8,128)(2,1)}, u32[]{:S(2)}) %copy-start.4) | copy-done | bytes 1572888
  21.4 0.3 fusion.20
  21.7 1.0 %fusion.11 = f32[768,1024]{1,0:T(8,128)S(1)} fusion(bf16[768,512]{0,1:T(8,128)(2,1)S(1)} %multiply_convert_fusion.1, bf16[512,1536]{1,0:T(8,128)(2,1)S(1)} %copy-done.4), kind=kOutput, calls=%fused_computation.23 | convolution fusion | flops 805306368 | bytes 4980736 | tf_op jit(solution)/shard_map/dot_general | solution.py:122
  22.9 1.3 %slice.28 = f32[768,512]{1,0:T(8,128)} slice(f32[768,1024]{1,0:T(8,128)S(1)} %fusion.11), slice={[0:768], [0:512]} | slice | bytes 3145728 | tf_op jit(solution)/shard_map/slice | solution.py:123
  24.4 0.3 multiply_reduce_fusion.4
  24.7 1.0 %multiply_convert_fusion.4 = bf16[256,4,128]{2,1,0:T(4,128)(2,1)} fusion(f32[256,4,128]{2,1,0:T(4,128)S(1)} %reshape.154, f32[256,4]{1,0:T(8,128)S(1)} %add_rsqrt_fusion.1), kind=kLoop, calls=%fused_computation.37 | loop fusion | flops 262144 | bytes 790528 | tf_op jit(solution)/shard_map/convert_element_type | solution.py:56
  25.8 1.8 %reshape.155 = f32[768,4,128]{2,1,0:T(4,128)S(1)} reshape(f32[768,512]{1,0:T(8,128)} %slice.28) | data formatting | bytes 3145728 | tf_op jit(solution)/shard_map/reshape | solution.py:55
  27.6 1.2 %copy.49 = bf16[768,512]{0,1:T(8,128)(2,1)} copy(bf16[768,512]{1,0:T(8,128)(2,1)S(1)} %slice.46) | data formatting | bytes 1572864 | tf_op jit(solution)/shard_map/reshape | solution.py:124
  28.7 0.9 %multiply_reduce_fusion = f32[768,4]{1,0:T(8,128)S(1)} fusion(f32[768,4,128]{2,1,0:T(4,128)S(1)} %reshape.155), kind=kLoop, calls=%fused_computation.7 | loop fusion | flops 783360 | bytes 1585152 | tf_op jit(solution)/shard_map/reduce_sum | solution.py:51
  29.7 1.0 %multiply_convert_fusion = bf16[768,4,128]{2,1,0:T(4,128)(2,1)S(1)} fusion(f32[768,4,128]{2,1,0:T(4,128)S(1)} %reshape.155, f32[768,4]{1,0:T(8,128)S(1)} %add_rsqrt_fusion), kind=kLoop, calls=%fused_computation.6 | loop fusion | flops 786432 | bytes 2371584 | tf_op jit(solution)/shard_map/convert_element_type | solution.py:56
  30.9 1.0 %fusion = (f32[4,256]{1,0:T(4,128)S(1)}, f32[4,256,768]{2,1,0:T(8,128)S(1)}) fusion(f32[256,768]{1,0:T(8,128)S(1)} %copy-done.3, bf16[768,4,128]{2,1,0:T(4,128)(2,1)S(1)} %multiply_convert_fusion, bf16[256,4,128]{2,1,0:T(4,128)(2,1)S(1)} %copy-done.5), kind=kOutput, calls=%fused_computation.3 | convolution fusion | flops 203684864 | bytes 4984832 | tf_op jit(solution)/shard_map/qhd,khd->hqk/dot_general | solution.py:74
  32.0 0.9 %fusion.2 = bf16[4,128,256]{2,1,0:T(8,128)(2,1)S(1)} fusion(bf16[768,4,128]{0,2,1:T(8,128)(2,1)S(1)} %bitcast.37, f32[4,256,768]{2,1,0:T(8,128)S(1)} %get-tuple-element.39, f32[4,256]{1,0:T(4,128)S(1)} %get-tuple-element.38, f32[256,768]{1,0:T(8,128)S(1)} %copy-done.3), kind=kOutput, calls=%fused_computation.13 | convolution fusion | flops 204603392 | bytes 4984832 | tf_op jit(solution)/shard_map/hqk,khd->qhd/dot_general | solution.py:83
  32.9 0.5 copy-done.2
  33.5 0.4 multiply_reduce_fusion.3
  33.9 3.2 %multiply_reduce_fusion.2 = (f32[256]{0:T(256)S(1)}, f32[256,512]{0,1:T(8,128)}) fusion(bf16[1024,512]{1,0:T(8,128)(2,1)S(1)} %copy-done, bf16[512,1024]{1,0:T(8,128)(2,1)} %param.21, f32[256]{0:T(256)S(1)} %add_rsqrt_fusion.4, f32[256,512]{0,1:T(8,128)S(1)} %get-tuple-element.41, f32[768,512]{0,1:T(8,128)S(1)} %copy-done.2), kind=kOutput, calls=%fused_computation.30 | convolution fusion | flops 540147456 | bytes 4720640 | tf_op jit(solution)/shard_map/dot_general | solution.py:95
  37.2 1.9 %convolution_multiply_fusion = f32[256,84]{0,1:T(8,128)S(1)} fusion(bf16[512,84]{0,1:T(8,128)(2,1)S(1)} %copy-done.11, f32[256,512]{0,1:T(8,128)} %get-tuple-element.43, f32[256]{0:T(256)S(1)} %add_rsqrt_fusion.3, f32[]{:T(128)} %fusion.30), kind=kOutput, calls=%fused_computation.14 | convolution fusion | flops 22303744 | bytes 697348 | tf_op jit(solution)/shard_map/dot_general | solution.py:96
  39.5 15.1 %all_gather.3 = f32[4,2,10752]{2,1,0:T(2,128)S(1)} all-gather(f32[1,2,10752]{2,1,0:T(2,128)S(1)} %mul.182), channel_id=1, replica_groups=mesh['step'=4,'band'=8] {'step'}, dimensions={0}, use_global_device_ids=true | all-gather | bytes 430080 | tf_op jit(solution)/shard_map/all_gather | solution.py:41
  54.7 1.3 %fusion.28 = (f32[]{:T(128)}, f32[1,2,10752]{2,1,0:T(2,128)}) fusion(f32[1,2,10752]{2,1,0:T(2,128)S(1)} %copy-done.8, f32[2]{0:T(128)S(1)} %add_cosine_fusion, f32[2,10752]{1,0:T(2,128)S(1)} %copy-done.9, f32[2,10752]{1,0:T(2,128)S(1)} %get-tuple-element.25, f32[2,10752]{1,0:T(2,128)S(1)} %mul.183), kind=kLoop, calls=%fused_computation.50 | loop fusion | flops 129023 | bytes 430092 | tf_op jit(solution)/shard_map/reduce_sum | solution.py:147
  56.0 12.4 %psum.7 = f32[1]{0:T(128)} all-reduce(f32[1]{0:T(128)} %bitcast.7), channel_id=1, replica_groups=mesh['step'=4,'band'=8] {'band'}, use_global_device_ids=true, to_apply=%region_10.11 | all-reduce | flops 1 | bytes 8 | tf_op jit(solution)/shard_map/psum | solution.py:148
  (44 shorter events, 1.8 us)
Async XLA Ops:
  0.6 33.3 %copy-start = (bf16[1024,512]{1,0:T(8,128)(2,1)S(1)}, bf16[1024,512]{1,0:T(8,128)(2,1)}, u32[]{:S(2)}) copy-start(bf16[1024,512]{1,0:T(8,128)(2,1)} %param.22) | copy-start | bytes 3145732
  1.7 8.3 %collective-permute-start = (bf16[1,2,10752]{2,1,0:T(2,128)(2,1)S(1)}, bf16[1,2,10752]{2,1,0:T(2,128)(2,1)S(1)}, u32[]{:S(2)}, u32[]{:S(2)}) collective-permute-start(bf16[1,2,10752]{2,1,0:T(2,128)(2,1)S(1)} %convert_element_type.52), channel_id=1, source_target_pairs={{0,8},{8,16},{16,24},{1,9},{9,17},{17,25},{2,10},{10,18},{18,26},{... | collective-permute-start | bytes 129032 | tf_op jit(solution)/shard_map/ppermute | solution.py:23
  10.9 7.3 %collective-permute-start.2 = (bf16[1,2,10752]{2,1,0:T(2,128)(2,1)S(1)}, bf16[1,2,10752]{2,1,0:T(2,128)(2,1)S(1)}, u32[]{:S(2)}, u32[]{:S(2)}) collective-permute-start(bf16[1,2,10752]{2,1,0:T(2,128)(2,1)S(1)} %fusion.29), channel_id=1, source_target_pairs={{1,0},{2,1},{3,2},{4,3},{5,4},{6,5},{7,6},{9,8},{10,9},{11,10},{12... | collective-permute-start | bytes 129032 | tf_op jit(solution)/shard_map/ppermute | solution.py:34
  12.2 6.0 %collective-permute-start.1 = (bf16[1,2,10752]{2,1,0:T(2,128)(2,1)S(1)}, bf16[1,2,10752]{2,1,0:T(2,128)(2,1)S(1)}, u32[]{:S(2)}, u32[]{:S(2)}) collective-permute-start(bf16[1,2,10752]{2,1,0:T(2,128)(2,1)S(1)} %fusion.29), channel_id=1, source_target_pairs={{0,1},{1,2},{2,3},{3,4},{4,5},{5,6},{6,7},{8,9},{9,10},{10,11},{11... | collective-permute-start | bytes 129032 | tf_op jit(solution)/shard_map/ppermute | solution.py:33
  15.6 3.3 %copy-start.10 = (bf16[84,512]{1,0:T(8,128)(2,1)S(1)}, bf16[84,512]{1,0:T(8,128)(2,1)}, u32[]{:S(2)}) copy-start(bf16[84,512]{1,0:T(8,128)(2,1)} %param.17) | copy-start | bytes 258052
  19.4 1.2 %copy-start.1 = (f32[768,512]{0,1:T(8,128)}, f32[768,512]{0,1:T(8,128)S(1)}, u32[]{:S(2)}) copy-start(f32[768,512]{0,1:T(8,128)S(1)} %get-tuple-element.37) | copy-start | bytes 4718596
  19.4 2.0 %copy-start.4 = (bf16[512,1536]{1,0:T(8,128)(2,1)S(1)}, bf16[512,1536]{1,0:T(8,128)(2,1)}, u32[]{:S(2)}) copy-start(bf16[512,1536]{1,0:T(8,128)(2,1)} %param.19) | copy-start | bytes 4718596
  29.7 1.1 %copy-start.3 = (f32[256,768]{1,0:T(8,128)S(1)}, f32[256,768]{1,0:T(8,128)}, u32[]{:S(2)}) copy-start(f32[256,768]{1,0:T(8,128)} %copy.41) | copy-start | bytes 2359300
  29.7 1.2 %copy-start.5 = (bf16[256,4,128]{2,1,0:T(4,128)(2,1)S(1)}, bf16[256,4,128]{2,1,0:T(4,128)(2,1)}, u32[]{:S(2)}) copy-start(bf16[256,4,128]{2,1,0:T(4,128)(2,1)} %multiply_convert_fusion.4) | copy-start | bytes 786436
  30.9 1.1 %copy-start.6 = (bf16[768,512]{0,1:T(8,128)(2,1)S(1)}, bf16[768,512]{0,1:T(8,128)(2,1)}, u32[]{:S(2)}) copy-start(bf16[768,512]{0,1:T(8,128)(2,1)} %copy.49) | copy-start | bytes 2359300
  32.0 1.4 %copy-start.2 = (f32[768,512]{0,1:T(8,128)S(1)}, f32[768,512]{0,1:T(8,128)}, u32[]{:S(2)}) copy-start(f32[768,512]{0,1:T(8,128)} %copy-done.1) | copy-start | bytes 4718596
  32.0 1.5 %copy-start.7 = (bf16[512,512]{1,0:T(8,128)(2,1)S(1)}, bf16[512,512]{1,0:T(8,128)(2,1)}, u32[]{:S(2)}) copy-start(bf16[512,512]{1,0:T(8,128)(2,1)} %param.20) | copy-start | bytes 1572868
  33.9 3.2 %copy-start.11 = (bf16[512,84]{0,1:T(8,128)(2,1)S(1)}, bf16[512,84]{0,1:T(8,128)(2,1)}, u32[]{:S(2)}) copy-start(bf16[512,84]{0,1:T(8,128)(2,1)} %param.23) | copy-start | bytes 258052
  37.1 17.5 %copy-start.8 = (f32[1,2,10752]{2,1,0:T(2,128)S(1)}, f32[1,2,10752]{2,1,0:T(2,128)}, u32[]{:S(2)}) copy-start(f32[1,2,10752]{2,1,0:T(2,128)} %param.13) | copy-start | bytes 258052
  37.2 17.5 %copy-start.9 = (f32[2,10752]{1,0:T(2,128)S(1)}, f32[2,10752]{1,0:T(2,128)}, u32[]{:S(2)}) copy-start(f32[2,10752]{1,0:T(2,128)} %param.14) | copy-start | bytes 258052
where the time goes:
time: 70.7 us; the launch traced here: 70.2 us
  blocking collectives  27.5 us (39%)
  local copies, waits for them, and re-layouts  10 us (14%)
  other arithmetic  9.62 us (14%)
  starting transfers between devices  9.25 us (13%)
  matrix products  9.07 us (13%)
  between operations  4.69 us (7%)
    all_gather x1, blocking collectives, carried_in(): gathered = lax.all_gather(part, axis)  15.1 us
    psum x1, blocking collectives, local(): change = lax.psum(partial_value, 'band') / (area_total * field_width)  12.4 us
    ppermute x1, starting transfers between devices, passed_along(): return lax.ppermute(array, axis, pairs)  4.93 us
    dot_general x1, matrix products, finish_block(): mixed = mixed + jnp.dot(hidden, down_w, preferred_element_type=jnp.float32)  3.2 us
    ppermute x1, starting transfers between devices, with_halo(): before = lax.ppermute(last, axis, up)  3.03 us
    unnamed x25, local copies, waits for them, and re-layouts  2.81 us
    convert_element_type x2, other arithmetic, split_heads(): return heads.astype(jnp.bfloat16)  2.07 us
    reshape x2, local copies, waits for them, and re-layouts, split_heads(): heads = rms_scale(projected.reshape(projected.shape[0], HEADS, HEAD_DIM))  1.96 us
  transfers between devices with their start and end apart: 3, of which 0 were waited for; matrix products, arithmetic and copies ran while one was open for 6% of the time, Pallas kernels for 0%

commit v1 on v0

v1 whole, which is shorter than its diff:
```python
import functools
import math

import jax
import jax.numpy as jnp
import numpy as np
from jax import lax
from jax.experimental import pallas as pl
from jax.experimental.pallas import tpu as pltpu
from jax.sharding import PartitionSpec as P

HEADS = 4
R = 2
LANES = 128
CHUNKS = 3

epsilon = 1e-06
score_gain = 3.0

MESH = pl.DeviceIdType.MESH


def rms_scale(values):
    return values * lax.rsqrt(jnp.mean(values * values, axis=-1, keepdims=True) + epsilon)


def dot(a, b):
    return jnp.dot(a, b, preferred_element_type=jnp.float32)


def kernel(
    sizes,
    step_index, sigmas, states_hbm, anchor_hbm, enc_hbm, embed_hbm, qkv_hbm, out_hbm, up_hbm,
    down_hbm, dec_hbm,
    new_ref, change_ref,
    states_flat, anchor_flat, enc_w, noise_embed, qkv_w, out_w, up_w, down_w, dec_w,
    states_rows, anchor_rows, sent, fields, keys, values, attended, padded,
    carry_in, carry_out, partials, load_sem, sent_sem, fields_sem, carry_send, carry_recv,
    part_send, part_recv,
):
    steps, bands = sizes
    step, band = lax.axis_index("step"), lax.axis_index("band")
    lat_rows, width = states_flat.shape
    channels, model = enc_w.shape
    columns = width // channels
    tokens = lat_rows * columns
    groups = width // LANES
    rows = states_rows.shape[0]
    padded_rows = sent.shape[0]
    head = model // HEADS
    above, below = band > 0, band < bands - 1
    opens, closes = step == 0, step == steps - 1

    pairs = (
        (states_hbm.at[0], states_flat), (anchor_hbm, anchor_flat), (enc_hbm, enc_w),
        (embed_hbm, noise_embed), (qkv_hbm, qkv_w), (out_hbm, out_w), (up_hbm, up_w),
        (down_hbm, down_w), (dec_hbm, dec_w),
    )
    loads = [pltpu.make_async_copy(a, b, load_sem.at[i]) for i, (a, b) in enumerate(pairs)]
    for load in loads:
        load.start()

    barrier = pltpu.get_barrier_semaphore()

    def greet(to_step, to_band):
        pl.semaphore_signal(barrier, inc=1, device_id=(to_step, to_band), device_id_type=MESH)

    @pl.when(step > 0)
    def _():
        greet(step - 1, band)

        @pl.when(above)
        def _():
            greet(step - 1, band - 1)

        @pl.when(below)
        def _():
            greet(step - 1, band + 1)

    for d in range(1, bands):
        greet(step, lax.rem(band + d, bands))

    def to_rows(flat, out):
        for g in range(groups):
            out[lat_rows * g : lat_rows * (g + 1), :] = flat[:, LANES * g : LANES * (g + 1)]

    loads[0].wait()
    to_rows(states_flat, states_rows)
    zero_rows = jnp.zeros((padded_rows - rows, LANES), jnp.float32)
    sent[...] = jnp.concatenate([states_rows[...], zero_rows], axis=0).astype(jnp.bfloat16)
    loads[1].wait()
    to_rows(anchor_flat, anchor_rows)

    @pl.when(opens)
    def _():
        fields[1] = jnp.concatenate([anchor_rows[...], zero_rows], axis=0).astype(jnp.bfloat16)

    onward = 1 + above.astype(jnp.int32) + below.astype(jnp.int32)
    pl.semaphore_wait(barrier, bands - 1 + jnp.where(closes, 0, onward))

    def field_copy(source, slot, sem, to_step, to_band):
        return pltpu.make_async_remote_copy(
            src_ref=source, dst_ref=fields.at[slot], send_sem=sent_sem.at[sem],
            recv_sem=fields_sem.at[slot], device_id=(to_step, to_band), device_id_type=MESH,
        )

    to_center = field_copy(sent, 1, 0, step + 1, band)
    to_above = field_copy(sent, 2, 1, step + 1, band - 1)
    to_below = field_copy(sent, 0, 2, step + 1, band + 1)
    open_above = field_copy(fields.at[1], 2, 3, step, band - 1)
    open_below = field_copy(fields.at[1], 0, 4, step, band + 1)

    def for_fields(act):
        @pl.when(jnp.logical_not(closes))
        def _():
            act(to_center)

            @pl.when(above)
            def _():
                act(to_above)

            @pl.when(below)
            def _():
                act(to_below)

        @pl.when(opens)
        def _():
            @pl.when(above)
            def _():
                act(open_above)

            @pl.when(below)
            def _():
                act(open_below)

    for_fields(lambda copy: copy.start())

    @pl.when(jnp.logical_not(above))
    def _():
        fields[0] = jnp.zeros((padded_rows, LANES), jnp.bfloat16)

    @pl.when(jnp.logical_not(below))
    def _():
        fields[2] = jnp.zeros((padded_rows, LANES), jnp.bfloat16)

    unit = math.gcd(channels, LANES)
    period = LANES // unit
    stride = pow(-(channels // unit), -1, period)

    def column_of(token):
        place, turn = token % columns, token % period
        return place - turn + (turn * stride) % period

    def places(shape, token_dim, row_dim, later):
        token = lax.broadcasted_iota(jnp.int32, shape, token_dim)
        row = lax.broadcasted_iota(jnp.int32, shape, row_dim)
        lat, column = token // columns, column_of(token)
        first = (column * channels) // LANES + later
        return (row == first * lat_rows + lat).astype(jnp.float32).astype(jnp.bfloat16)

    gather_first = places((tokens, padded_rows), 0, 1, 0)
    gather_next = places((tokens, padded_rows), 0, 1, 1)
    token = lax.broadcasted_iota(jnp.int32, (tokens, LANES), 0)
    lane = lax.broadcasted_iota(jnp.int32, (tokens, LANES), 1)
    in_first = lane >= (column_of(token) * channels) % LANES

    noise = sigmas[step_index[0]]
    loads[2].wait()
    loads[3].wait()
    offset = jnp.log(jnp.full((1, model), noise, jnp.float32)) * noise_embed[...].reshape(1, model)
    loads[4].wait()

    def embed(slot):
        packed = fields[slot]
        picked = jnp.where(in_first, dot(gather_first, packed), dot(gather_next, packed))
        turned = pltpu.roll(picked, 0, 1, stride=unit, stride_axis=0)
        return dot(turned[:, :channels].astype(jnp.bfloat16), enc_w[...]) + offset

    def keep_key_value(slot, key_value, valid):
        at = slice(slot * tokens, (slot + 1) * tokens)
        for h in range(HEADS):
            here = slice(h * head, (h + 1) * head)
            keys[at, here] = rms_scale(key_value[:, here]).astype(jnp.bfloat16)
            value = key_value[:, model + h * head : model + (h + 1) * head]
            ones = jnp.ones((tokens, head), jnp.float32)
            if valid is not None:
                value, ones = value * valid, ones * valid
            values[at, 2 * h * head : (2 * h + 1) * head] = value.astype(jnp.bfloat16)
            values[at, (2 * h + 1) * head : (2 * h + 2) * head] = ones.astype(jnp.bfloat16)

    @pl.when(jnp.logical_not(opens))
    def _():
        to_center.wait_recv()

    embedded = embed(1)
    projected = dot(rms_scale(embedded).astype(jnp.bfloat16), qkv_w[...])
    queries = [
        rms_scale(projected[:, h * head : (h + 1) * head]).astype(jnp.bfloat16)
        for h in range(HEADS)
    ]
    keep_key_value(1, projected[:, model:], None)

    for slot, there, copy in ((0, above, to_below), (2, below, to_above)):
        pl.when(there)(copy.wait_recv)
        normed = rms_scale(embed(slot)).astype(jnp.bfloat16)
        keep_key_value(slot, dot(normed, qkv_w[:, model:]), there.astype(jnp.float32))

    gain = score_gain / math.sqrt(head) * math.log2(math.e)
    for h in range(HEADS):
        for i in range(lat_rows):
            window = slice(i * columns, (i + 2 * R + 1) * columns)
            mine = slice(i * columns, (i + 1) * columns)
            scores = lax.dot_general(
                queries[h][mine], keys[window, h * head : (h + 1) * head],
                (((1,), (1,)), ((), ())), preferred_element_type=jnp.float32,
            )
            weights = jnp.exp2(scores * gain).astype(jnp.bfloat16)
            sums = dot(weights, values[window, 2 * h * head : (2 * h + 2) * head])
            attended[mine, h * head : (h + 1) * head] = (
                sums[:, :head] / sums[:, head:]
            ).astype(jnp.bfloat16)

    loads[5].wait()
    mixed = embedded + dot(attended[...], out_w[...])
    loads[6].wait()
    hidden = jax.nn.gelu(dot(rms_scale(mixed).astype(jnp.bfloat16), up_w[...]))
    loads[7].wait()
    mixed = mixed + dot(hidden.astype(jnp.bfloat16), down_w[...])
    loads[8].wait()
    padded[...] = jnp.zeros_like(padded)
    padded[:, :channels] = lax.dot_general(
        rms_scale(mixed).astype(jnp.bfloat16), dec_w[...], (((1,), (1,)), ((), ())),
        preferred_element_type=jnp.float32,
    )

    turned = padded[...]
    turns = (period - token % period) % period
    for bit in range((period - 1).bit_length()):
        turned = jnp.where((turns >> bit) % 2 == 1, pltpu.roll(turned, unit << bit, 1), turned)
    split = jnp.concatenate(
        [jnp.where(in_first, turned, 0.0), jnp.where(in_first, 0.0, turned)], axis=0
    )
    coarse = split.astype(jnp.bfloat16)
    fine = (split - coarse.astype(jnp.float32)).astype(jnp.bfloat16)
    scatter = jnp.concatenate(
        [places((padded_rows, tokens), 1, 0, 0), places((padded_rows, tokens), 1, 0, 1)], axis=1
    )
    both = dot(scatter, jnp.concatenate([coarse, fine], axis=1))
    own = noise * (both[:rows, :LANES] + both[:rows, LANES:])

    piece = rows // CHUNKS
    carries = []
    for c in range(CHUNKS):
        at = slice(c * piece, (c + 1) * piece)
        carries.append(
            pltpu.make_async_remote_copy(
                src_ref=carry_out.at[at], dst_ref=carry_in.at[at], send_sem=carry_send.at[c],
                recv_sem=carry_recv.at[c], device_id=(step + 1, band), device_id_type=MESH,
            )
        )

    @pl.when(opens)
    def _():
        carry_in[...] = jnp.zeros_like(carry_in)

    partial = jnp.zeros((8, LANES), jnp.float32)
    for c, carry in enumerate(carries):
        at = slice(c * piece, (c + 1) * piece)
        pl.when(jnp.logical_not(opens))(carry.wait_recv)
        carry_out[at] = carry_in[at] + own[at]
        pl.when(jnp.logical_not(closes))(carry.start)
        renewed = anchor_rows[at] + carry_out[at]
        mismatch = renewed - states_rows[at]
        partial += jnp.sum((mismatch * mismatch).reshape(piece // 8, 8, LANES), axis=0)
        for g in range(c * piece // lat_rows, (c + 1) * piece // lat_rows):
            low = lat_rows * g - c * piece
            new_ref[0, :, LANES * g : LANES * (g + 1)] = renewed[low : low + lat_rows]

    total_rows = lat_rows * bands
    table = np.cos(np.pi * ((np.arange(total_rows) + 0.5) / total_rows - 0.5))
    lat = lax.broadcasted_iota(jnp.int32, (8, LANES), 0) % lat_rows + band * lat_rows
    area = jnp.zeros((8, LANES), jnp.float32)
    for i, value in enumerate(table):
        area = jnp.where(lat == i, float(value), area)
    partials[band] = partial * area

    parts = [
        pltpu.make_async_remote_copy(
            src_ref=partials.at[band], dst_ref=partials.at[band], send_sem=part_send.at[d - 1],
            recv_sem=part_recv.at[d - 1], device_id=(step, lax.rem(band + d, bands)),
            device_id_type=MESH,
        )
        for d in range(1, bands)
    ]
    for part in parts:
        part.start()
    for part in parts:
        part.wait_recv()
    total = jnp.sum(partials[...], axis=0)
    change_ref[0] = jnp.sum(total) * (1.0 / float(np.sum(table) * width))

    for part in parts:
        part.wait_send()
    for carry in carries:
        pl.when(jnp.logical_not(closes))(carry.wait_send)
    for_fields(lambda copy: copy.wait_send())


def local(
    sizes, states, anchor, step_index, sigmas, enc_w, noise_embed, qkv_w, out_w, up_w, down_w, dec_w
):
    _, lat_rows, width = states.shape
    channels, model = enc_w.shape
    columns = width // channels
    rows = lat_rows * width // LANES
    padded_rows = -(-rows // 16) * 16
    tokens = lat_rows * columns
    steps, bands = sizes
    f32, bf16 = jnp.float32, jnp.bfloat16
    weights = (enc_w, noise_embed, qkv_w, out_w, up_w, down_w, dec_w.T)
    hbm = pl.BlockSpec(memory_space=pl.ANY)
    smem = pl.BlockSpec(memory_space=pltpu.SMEM)
    dma = pltpu.SemaphoreType.DMA
    return pl.pallas_call(
        functools.partial(kernel, sizes),
        out_shape=(
            jax.ShapeDtypeStruct(states.shape, f32),
            jax.ShapeDtypeStruct((1,), f32),
        ),
        in_specs=[smem, smem] + [hbm] * 9,
        out_specs=(pl.BlockSpec(memory_space=pltpu.VMEM), smem),
        scratch_shapes=[
            pltpu.VMEM((lat_rows, width), f32),
            pltpu.VMEM((lat_rows, width), f32),
        ]
        + [pltpu.VMEM(w.shape, w.dtype) for w in weights]
        + [
            pltpu.VMEM((rows, LANES), f32),
            pltpu.VMEM((rows, LANES), f32),
            pltpu.VMEM((padded_rows, LANES), bf16),
            pltpu.VMEM((3, padded_rows, LANES), bf16),
            pltpu.VMEM((3 * tokens, model), bf16),
            pltpu.VMEM((3 * tokens, 2 * model), bf16),
            pltpu.VMEM((tokens, model), bf16),
            pltpu.VMEM((tokens, LANES), f32),
            pltpu.VMEM((rows, LANES), f32),
            pltpu.VMEM((rows, LANES), f32),
            pltpu.VMEM((bands, 8, LANES), f32),
            dma((9,)),
            dma((5,)),
            dma((3,)),
            dma((CHUNKS,)),
            dma((CHUNKS,)),
            dma((bands - 1,)),
            dma((bands - 1,)),
        ],
        compiler_params=pltpu.CompilerParams(
            collective_id=0, has_side_effects=True, vmem_limit_bytes=48 * 1024 * 1024
        ),
        cost_estimate=pl.CostEstimate(flops=2 * 10**9, bytes_accessed=5 * 10**6, transcendentals=10**6),
    )(step_index, sigmas, states, anchor, *weights)


def solution(mesh):
    placed = (
        P("step", "band", None), P("band", None), P("step"),
        P(), P(), P(), P(), P(), P(), P(), P(),
    )
    return jax.shard_map(
        functools.partial(local, (mesh.shape["step"], mesh.shape["band"])),
        mesh=mesh,
        in_specs=placed,
        out_specs=(P("step", "band", None), P("step")),
        check_vma=False,
    )
```

time: 70.7 us -> 38.1 us (0.54)
  the two profiles are of different devices: /device:TPU:0 before, /device:TPU:25 now
where the time goes in v1:
time: 38.1 us; the launch traced here: 37.7 us
  Pallas kernels  24.2 us (64%)
  local copies, waits for them, and re-layouts  10.4 us (27%)
  between operations  3.07 us (8%)
    pallas_call x1, Pallas kernels, local(): pl.pallas_call(functools.partial(kernel, sizes), out_shape=(jax.ShapeDtyp...  24.2 us
    unnamed x21, local copies, waits for them, and re-layouts  10.4 us

profile of v1, /device:TPU:25, one launch (start us, length us, event | category | flops | bytes accessed | tf_op | source)
XLA Modules:
  0.0 37.7 jit_solution(6957265544183460481)
XLA Ops:
  1.3 0.0 copy-start
  1.3 1.4 %copy-done = bf16[512,1536]{1,0:T(8,128)(2,1)S(1)} copy-done((bf16[512,1536]{1,0:T(8,128)(2,1)S(1)}, bf16[512,1536]{1,0:T(8,128)(2,1)}, u32[]{:S(2)}) %copy-start) | copy-done | bytes 1572888
  2.7 0.0 copy-start.1
  2.7 1.2 %copy-done.1 = bf16[512,1024]{1,0:T(8,128)(2,1)S(1)} copy-done((bf16[512,1024]{1,0:T(8,128)(2,1)S(1)}, bf16[512,1024]{1,0:T(8,128)(2,1)}, u32[]{:S(2)}) %copy-start.1) | copy-done | bytes 1048600
  3.9 0.0 copy-start.2
  3.9 1.2 %copy-done.2 = bf16[1024,512]{1,0:T(8,128)(2,1)S(1)} copy-done((bf16[1024,512]{1,0:T(8,128)(2,1)S(1)}, bf16[1024,512]{1,0:T(8,128)(2,1)}, u32[]{:S(2)}) %copy-start.2) | copy-done | bytes 1048600
  5.1 0.0 copy-start.3
  5.1 1.0 %copy-done.3 = bf16[512,512]{1,0:T(8,128)(2,1)S(1)} copy-done((bf16[512,512]{1,0:T(8,128)(2,1)S(1)}, bf16[512,512]{1,0:T(8,128)(2,1)}, u32[]{:S(2)}) %copy-start.3) | copy-done | bytes 524312
  6.2 0.0 copy-start.4
  6.2 0.9 %copy-done.4 = bf16[84,512]{1,0:T(8,128)(2,1)S(1)} copy-done((bf16[84,512]{1,0:T(8,128)(2,1)S(1)}, bf16[84,512]{1,0:T(8,128)(2,1)}, u32[]{:S(2)}) %copy-start.4) | copy-done | bytes 86040
  7.1 0.0 copy-start.5
  7.1 0.9 %copy-done.5 = bf16[512,84]{0,1:T(8,128)(2,1)S(1)} copy-done((bf16[512,84]{0,1:T(8,128)(2,1)S(1)}, bf16[512,84]{0,1:T(8,128)(2,1)}, u32[]{:S(2)}) %copy-start.5) | copy-done | bytes 86040
  8.0 0.0 copy-start.6
  8.0 0.9 %copy-done.6 = f32[1,2,10752]{2,1,0:T(2,128)S(1)} copy-done((f32[1,2,10752]{2,1,0:T(2,128)S(1)}, f32[1,2,10752]{2,1,0:T(2,128)}, u32[]{:S(2)}) %copy-start.6) | copy-done | bytes 86040
  8.9 0.0 copy-start.7
  8.9 0.9 %copy-done.7 = f32[2,10752]{1,0:T(2,128)S(1)} copy-done((f32[2,10752]{1,0:T(2,128)S(1)}, f32[2,10752]{1,0:T(2,128)}, u32[]{:S(2)}) %copy-start.7) | copy-done | bytes 86040
  9.7 0.0 copy-start.8
  9.7 0.7 %copy-done.8 = f32[512]{0:T(512)S(1)} copy-done((f32[512]{0:T(512)S(1)}, f32[512]{0:T(512)}, u32[]{:S(2)}) %copy-start.8) | copy-done | bytes 2072
  10.4 0.0 copy-start.9
  10.4 0.7 %copy-done.9 = f32[20]{0:T(128)S(1)} copy-done((f32[20]{0:T(128)S(1)}, f32[20]{0:T(128)}, u32[]{:S(2)}) %copy-start.9) | copy-done | bytes 104
  11.1 24.2 %shard_map.122 = (f32[1,2,10752]{2,1,0:T(2,128)S(1)}, f32[1]{0:T(128)}) custom-call(s32[1]{0:T(128)S(6)} %copy.15.step_index, f32[20]{0:T(128)S(1)} %copy-done.9, f32[1,2,10752]{2,1,0:T(2,128)S(1)} %copy-done.6, f32[2,10752]{1,0:T(2,128)S(1)} %copy-done.7, bf16[84,512]{1,0:T(8,128)(2,1)S(1)} %copy-done.4, f32[512]{0:T(512)S(1)} %copy-done.8, ...), custom_call_target="tpu_custom_call" | custom-call | flops 2000000000 | bytes 5000000 | tf_op jit(solution)/shard_map/pallas_call | solution.py:324
  35.3 0.6 %copy.16 = f32[1,2,10752]{2,1,0:T(2,128)} copy(f32[1,2,10752]{2,1,0:T(2,128)S(1)} %get-tuple-element.4) | data formatting | bytes 172032
Async XLA Ops:
  1.3 1.4 %copy-start = (bf16[512,1536]{1,0:T(8,128)(2,1)S(1)}, bf16[512,1536]{1,0:T(8,128)(2,1)}, u32[]{:S(2)}) copy-start(bf16[512,1536]{1,0:T(8,128)(2,1)} %qkv_hbm.1) | copy-start | bytes 4718596
  2.7 1.2 %copy-start.1 = (bf16[512,1024]{1,0:T(8,128)(2,1)S(1)}, bf16[512,1024]{1,0:T(8,128)(2,1)}, u32[]{:S(2)}) copy-start(bf16[512,1024]{1,0:T(8,128)(2,1)} %up_hbm.1) | copy-start | bytes 3145732
  3.9 1.2 %copy-start.2 = (bf16[1024,512]{1,0:T(8,128)(2,1)S(1)}, bf16[1024,512]{1,0:T(8,128)(2,1)}, u32[]{:S(2)}) copy-start(bf16[1024,512]{1,0:T(8,128)(2,1)} %down_hbm.1) | copy-start | bytes 3145732
  5.1 1.0 %copy-start.3 = (bf16[512,512]{1,0:T(8,128)(2,1)S(1)}, bf16[512,512]{1,0:T(8,128)(2,1)}, u32[]{:S(2)}) copy-start(bf16[512,512]{1,0:T(8,128)(2,1)} %out_hbm.1) | copy-start | bytes 1572868
  6.2 0.9 %copy-start.4 = (bf16[84,512]{1,0:T(8,128)(2,1)S(1)}, bf16[84,512]{1,0:T(8,128)(2,1)}, u32[]{:S(2)}) copy-start(bf16[84,512]{1,0:T(8,128)(2,1)} %enc_hbm.1) | copy-start | bytes 258052
  7.1 0.9 %copy-start.5 = (bf16[512,84]{0,1:T(8,128)(2,1)S(1)}, bf16[512,84]{0,1:T(8,128)(2,1)}, u32[]{:S(2)}) copy-start(bf16[512,84]{0,1:T(8,128)(2,1)} %param.21) | copy-start | bytes 258052
  8.0 0.9 %copy-start.6 = (f32[1,2,10752]{2,1,0:T(2,128)S(1)}, f32[1,2,10752]{2,1,0:T(2,128)}, u32[]{:S(2)}) copy-start(f32[1,2,10752]{2,1,0:T(2,128)} %states_hbm.1) | copy-start | bytes 258052
  8.9 0.9 %copy-start.7 = (f32[2,10752]{1,0:T(2,128)S(1)}, f32[2,10752]{1,0:T(2,128)}, u32[]{:S(2)}) copy-start(f32[2,10752]{1,0:T(2,128)} %anchor_hbm.1) | copy-start | bytes 258052
  9.7 0.7 %copy-start.8 = (f32[512]{0:T(512)S(1)}, f32[512]{0:T(512)}, u32[]{:S(2)}) copy-start(f32[512]{0:T(512)} %embed_hbm.1) | copy-start | bytes 6148
  10.4 0.7 %copy-start.9 = (f32[20]{0:T(128)S(1)}, f32[20]{0:T(128)}, u32[]{:S(2)}) copy-start(f32[20]{0:T(128)} %sigmas.1) | copy-start | bytes 244

commit v2 on v1

--- a/solution.py
+++ b/solution.py
@@ -12,7 +12,7 @@
 HEADS = 4
 R = 2
 LANES = 128
-CHUNKS = 3
+CHUNKS = 7
 
 epsilon = 1e-06
 score_gain = 3.0
@@ -355,7 +355,7 @@
             dma((bands - 1,)),
         ],
         compiler_params=pltpu.CompilerParams(
-            collective_id=0, has_side_effects=True, vmem_limit_bytes=48 * 1024 * 1024
+            collective_id=0, has_side_effects=True, vmem_limit_bytes=64 * 1024 * 1024
         ),
         cost_estimate=pl.CostEstimate(flops=2 * 10**9, bytes_accessed=5 * 10**6, transcendentals=10**6),
     )(step_index, sigmas, states, anchor, *weights)

time: 38.1 us -> 28.2 us (0.74)
  local copies, waits for them, and re-layouts: 10.4 us -> 1.53 us
  Pallas kernels: 24.2 us -> 23.4 us
    unnamed x21 -> x1, local copies, waits for them, and re-layouts: 10.4 us -> 1.53 us
    pallas_call x1, Pallas kernels: 24.2 us -> 23.4 us  [local(): pl.pallas_call(functools.partial(kernel, sizes), out_shape=(jax.ShapeDtyp...]
where the time goes in v2:
time: 28.2 us; the launch traced here: 28 us
  Pallas kernels  23.4 us (83%)
  between operations  3.11 us (11%)
  local copies, waits for them, and re-layouts  1.53 us (5%)
    pallas_call x1, Pallas kernels, local(): pl.pallas_call(functools.partial(kernel, sizes), out_shape=(jax.ShapeDtyp...  23.4 us
    unnamed x1, local copies, waits for them, and re-layouts  1.53 us

profile of v2, /device:TPU:25, one launch (start us, length us, event | category | flops | bytes accessed | tf_op | source)
XLA Modules:
  0.0 28.0 jit_solution(9249192212381378411)
XLA Ops:
  1.3 23.4 %shard_map.122 = (f32[1,2,10752]{2,1,0:T(2,128)}, f32[1]{0:T(128)}) custom-call(s32[1]{0:T(128)S(6)} %copy.15.step_index, f32[20]{0:T(128)} %sigmas.1, f32[1,2,10752]{2,1,0:T(2,128)} %states_hbm.1, f32[2,10752]{1,0:T(2,128)} %anchor_hbm.1, bf16[84,512]{1,0:T(8,128)(2,1)} %enc_hbm.1, f32[512]{0:T(512)} %embed_hbm.1, bf16[512,1536]{1,0:T(8,128)(2,1)} %qkv_hbm.1, ...), custom_call_target="tpu_custom_call" | custom-call | flops 2000000000 | bytes 5000000 | tf_op jit(solution)/shard_map/pallas_call | solution.py:324
  24.7 1.5 %copy.16 = f32[1,2,10752]{2,1,0:T(2,128)} copy(f32[1,2,10752]{2,1,0:T(2,128)} %get-tuple-element.4) | data formatting | bytes 172032

commit v3 on v2

--- a/solution.py
+++ b/solution.py
@@ -324,7 +324,7 @@
     return pl.pallas_call(
         functools.partial(kernel, sizes),
         out_shape=(
-            jax.ShapeDtypeStruct(states.shape, f32),
+            pltpu.VMEM(states.shape, f32),
             jax.ShapeDtypeStruct((1,), f32),
         ),
         in_specs=[smem, smem] + [hbm] * 9,
@@ -355,7 +355,7 @@
             dma((bands - 1,)),
         ],
         compiler_params=pltpu.CompilerParams(
-            collective_id=0, has_side_effects=True, vmem_limit_bytes=64 * 1024 * 1024
+            collective_id=0, has_side_effects=True, vmem_limit_bytes=(65536 - 512) * 1024
         ),
         cost_estimate=pl.CostEstimate(flops=2 * 10**9, bytes_accessed=5 * 10**6, transcendentals=10**6),
     )(step_index, sigmas, states, anchor, *weights)

time: 28.2 us -> 27.1 us (0.961)
  local copies, waits for them, and re-layouts: 1.53 us -> 0.64 us
    unnamed x1, local copies, waits for them, and re-layouts: 1.53 us -> 0.64 us
where the time goes in v3:
time: 27.1 us; the launch traced here: 26.9 us
  Pallas kernels  23.3 us (86%)
  between operations  2.98 us (11%)
  local copies, waits for them, and re-layouts  0.64 us (2%)
    pallas_call x1, Pallas kernels, local(): pl.pallas_call(functools.partial(kernel, sizes), out_shape=(pltpu.VMEM(st...  23.3 us
    unnamed x1, local copies, waits for them, and re-layouts  0.64 us

profile of v3, /device:TPU:25, one launch (start us, length us, event | category | flops | bytes accessed | tf_op | source)
XLA Modules:
  0.0 26.9 jit_solution(13905717130646245669)
XLA Ops:
  1.3 23.3 %shard_map.122 = (f32[1,2,10752]{2,1,0:T(2,128)S(1)}, f32[1]{0:T(128)}) custom-call(s32[1]{0:T(128)S(6)} %copy.16.step_index, f32[20]{0:T(128)} %sigmas.1, f32[1,2,10752]{2,1,0:T(2,128)} %states_hbm.1, f32[2,10752]{1,0:T(2,128)} %anchor_hbm.1, bf16[84,512]{1,0:T(8,128)(2,1)} %enc_hbm.1, f32[512]{0:T(512)} %embed_hbm.1, bf16[512,1536]{1,0:T(8,128)(2,1)} %qkv_hbm.1, ...), custom_call_target="tpu_custom_call" | custom-call | flops 2000000000 | bytes 5000000 | tf_op jit(solution)/shard_map/pallas_call | solution.py:324
  24.6 0.6 %copy.15 = f32[1,2,10752]{2,1,0:T(2,128)} copy(f32[1,2,10752]{2,1,0:T(2,128)S(1)} %get-tuple-element.2) | data formatting | bytes 172032

commit v4 on v3

--- a/solution.py
+++ b/solution.py
@@ -200,22 +200,33 @@
     ]
     keep_key_value(1, projected[:, model:], None)
 
-    for slot, there, copy in ((0, above, to_below), (2, below, to_above)):
+    sides = ((0, above, to_below), (2, below, to_above))
+    normed = []
+    for slot, there, copy in sides:
         pl.when(there)(copy.wait_recv)
-        normed = rms_scale(embed(slot)).astype(jnp.bfloat16)
-        keep_key_value(slot, dot(normed, qkv_w[:, model:]), there.astype(jnp.float32))
+        normed.append(rms_scale(embed(slot)).astype(jnp.bfloat16))
+    key_value = dot(jnp.concatenate(normed, axis=0), qkv_w[:, model:])
+    for n, (slot, there, _) in enumerate(sides):
+        keep_key_value(slot, key_value[n * tokens : (n + 1) * tokens], there.astype(jnp.float32))
 
     gain = score_gain / math.sqrt(head) * math.log2(math.e)
+    def weigh(query, h, low, high):
+        window = slice(low * columns, high * columns)
+        scores = lax.dot_general(
+            query, keys[window, h * head : (h + 1) * head],
+            (((1,), (1,)), ((), ())), preferred_element_type=jnp.float32,
+        )
+        weights = jnp.exp2(scores * gain).astype(jnp.bfloat16)
+        return dot(weights, values[window, 2 * h * head : (2 * h + 2) * head])
+
     for h in range(HEADS):
+        shared = weigh(queries[h], h, lat_rows - 1, 2 * R + 1)
         for i in range(lat_rows):
-            window = slice(i * columns, (i + 2 * R + 1) * columns)
             mine = slice(i * columns, (i + 1) * columns)
-            scores = lax.dot_general(
-                queries[h][mine], keys[window, h * head : (h + 1) * head],
-                (((1,), (1,)), ((), ())), preferred_element_type=jnp.float32,
-            )
-            weights = jnp.exp2(scores * gain).astype(jnp.bfloat16)
-            sums = dot(weights, values[window, 2 * h * head : (2 * h + 2) * head])
+            sums = shared[mine]
+            for low, high in ((i, lat_rows - 1), (2 * R + 1, i + 2 * R + 1)):
+                if low < high:
+                    sums = sums + weigh(queries[h][mine], h, low, high)
             attended[mine, h * head : (h + 1) * head] = (
                 sums[:, :head] / sums[:, head:]
             ).astype(jnp.bfloat16)

time: 27.1 us -> 27 us (level)
  no operation moved by 1% of the time
where the time goes in v4:
time: 27 us; the launch traced here: 26.9 us
  Pallas kernels  23.2 us (86%)
  between operations  2.98 us (11%)
  local copies, waits for them, and re-layouts  0.64 us (2%)
    pallas_call x1, Pallas kernels, local(): pl.pallas_call(functools.partial(kernel, sizes), out_shape=(pltpu.VMEM(st...  23.2 us
    unnamed x1, local copies, waits for them, and re-layouts  0.64 us

profile of v4, /device:TPU:25, one launch (start us, length us, event | category | flops | bytes accessed | tf_op | source)
XLA Modules:
  0.0 26.9 jit_solution(6453847698229843942)
XLA Ops:
  1.3 23.2 %shard_map.122 = (f32[1,2,10752]{2,1,0:T(2,128)S(1)}, f32[1]{0:T(128)}) custom-call(s32[1]{0:T(128)S(6)} %copy.16.step_index, f32[20]{0:T(128)} %sigmas.1, f32[1,2,10752]{2,1,0:T(2,128)} %states_hbm.1, f32[2,10752]{1,0:T(2,128)} %anchor_hbm.1, bf16[84,512]{1,0:T(8,128)(2,1)} %enc_hbm.1, f32[512]{0:T(512)} %embed_hbm.1, bf16[512,1536]{1,0:T(8,128)(2,1)} %qkv_hbm.1, ...), custom_call_target="tpu_custom_call" | custom-call | flops 2000000000 | bytes 5000000 | tf_op jit(solution)/shard_map/pallas_call | solution.py:335
  24.5 0.6 %copy.15 = f32[1,2,10752]{2,1,0:T(2,128)} copy(f32[1,2,10752]{2,1,0:T(2,128)S(1)} %get-tuple-element.2) | data formatting | bytes 172032

commit v5 on v3

--- a/solution.py
+++ b/solution.py
@@ -12,7 +12,7 @@
 HEADS = 4
 R = 2
 LANES = 128
-CHUNKS = 7
+CHUNKS = 21
 
 epsilon = 1e-06
 score_gain = 3.0

time: 27.1 us -> 27.2 us (level)
  no operation moved by 1% of the time
where the time goes in v5:
time: 27.2 us; the launch traced here: 27 us
  Pallas kernels  23.4 us (86%)
  between operations  2.98 us (11%)
  local copies, waits for them, and re-layouts  0.64 us (2%)
    pallas_call x1, Pallas kernels, local(): pl.pallas_call(functools.partial(kernel, sizes), out_shape=(pltpu.VMEM(st...  23.4 us
    unnamed x1, local copies, waits for them, and re-layouts  0.64 us

profile of v5, /device:TPU:25, one launch (start us, length us, event | category | flops | bytes accessed | tf_op | source)
XLA Modules:
  0.0 27.0 jit_solution(9546999326363128008)
XLA Ops:
  1.3 23.4 %shard_map.122 = (f32[1,2,10752]{2,1,0:T(2,128)S(1)}, f32[1]{0:T(128)}) custom-call(s32[1]{0:T(128)S(6)} %copy.16.step_index, f32[20]{0:T(128)} %sigmas.1, f32[1,2,10752]{2,1,0:T(2,128)} %states_hbm.1, f32[2,10752]{1,0:T(2,128)} %anchor_hbm.1, bf16[84,512]{1,0:T(8,128)(2,1)} %enc_hbm.1, f32[512]{0:T(512)} %embed_hbm.1, bf16[512,1536]{1,0:T(8,128)(2,1)} %qkv_hbm.1, ...), custom_call_target="tpu_custom_call" | custom-call | flops 2000000000 | bytes 5000000 | tf_op jit(solution)/shard_map/pallas_call | solution.py:324
  24.7 0.6 %copy.15 = f32[1,2,10752]{2,1,0:T(2,128)} copy(f32[1,2,10752]{2,1,0:T(2,128)S(1)} %get-tuple-element.2) | data formatting | bytes 172032
